TPU v7x, 256 devices: a whole 4x4x8 slice. The times are simulated.
256 devices in a mesh: rel: 16 (over x, y), node: 16 (over z, core).
Axes of the slice: x: 4, y: 4, z: 8, core: 2. Of those that a mesh axis runs over, the one named last changes fastest.
Arguments:
- out_adjoint: bfloat16 [16, 1024, 512], P('node', 'rel'), may hold values from -6 to 6
- layer_input: bfloat16 [16, 1024, 512], P('node'), may hold values from -0.15625 to 0.15625
- rel_weights: bfloat16 [32, 512, 512], P('rel'), may hold values from -0.25 to 0.25
- self_weight: bfloat16 [512, 512], replicated, may hold values from -0.25 to 0.25
- tile_values: bfloat16 [16, 1024, 128, 128], P('rel', 'node'), may hold values from 0 to 0.039794922
- tile_rel: int32 [16, 1024], P('rel', 'node'), may hold values from 0 to 1
- tile_target: int32 [16, 1024], P('rel', 'node'), may hold values from 0 to 7
- tile_src: int32 [16, 1024], P('rel', 'node'), may hold values from 0 to 7
- tile_dest: int32 [16, 1024, 1], P('rel', 'node'), may hold values from 0 to 15; in each aligned block of 64 rows (0 to 63, 64 to 127, ..., all dimensions but the last counted through in order) at most 8 rows name the same one
Outputs:
- rel_weight_grad: float32 [32, 512, 512], P('rel', 'node')
- d_source: bfloat16 [16, 1024, 512], P('node', 'rel')
Inputs may be any that keep to these rules, and one draw needn't show every extreme that they name: `tile_dest`: among the 64 tiles of one device, at most 8 name the same node shard, and some node shard is named by exactly 8 of them.
All inputs are finite; a program needn't handle non-finite values.
Results may differ from a plain program's by a relative error of at most 0.0056.
Values may be sent and summed in bfloat16 or wider, within the bound.
A program may use at most 128 MiB of HBM per device.

v0:
```python
import jax
import jax.numpy as jnp
from jax import lax
from jax.sharding import PartitionSpec as P


def on_device(
    out_adjoint,
    layer_input,
    rel_weights,
    self_weight,
    tile_values,
    tile_rel,
    tile_target,
    tile_src,
    tile_dest,
):
    shard_count = lax.axis_size("node")
    tile_edge = tile_values.shape[-1]
    row_count = layer_input.shape[1]
    feature = layer_input.shape[2]
    blocks = row_count // tile_edge
    relations = rel_weights.shape[0]
    tile_count = tile_values.shape[1]
    capacity = 2 * tile_count // shard_count
    slot_count = shard_count * capacity
    adjoint = lax.all_gather(out_adjoint, "rel", axis=1, tiled=True)[0]
    owners = tile_dest[0, :, 0]
    relation = tile_rel[0]
    target = tile_target[0]
    source = tile_src[0]
    shared = owners[:, None] == owners[None, :]
    indices = jnp.arange(tile_count)
    earlier = indices[None, :] < indices[:, None]
    position = jnp.sum(jnp.logical_and(shared, earlier).astype(jnp.int32), axis=1)
    slot_of = owners * capacity + position
    placed = jnp.arange(slot_count)[:, None] == slot_of[None, :]
    placing = placed.astype(jnp.bfloat16)
    group_rows = lax.all_gather(adjoint[None], "node", axis=0, tiled=True)
    packed = relation * (blocks * blocks) + target * blocks + source
    outgoing = jnp.dot(
        placing,
        tile_values[0].reshape(tile_count, tile_edge * tile_edge),
        preferred_element_type=jnp.float32,
    )
    outgoing = outgoing.astype(jnp.bfloat16).reshape(shard_count, capacity, tile_edge, tile_edge)
    packed_slots = jnp.sum(jnp.where(placed, packed[None, :], 0), axis=1).reshape(
        shard_count, capacity
    )
    got_tiles, got_packed = (
        lax.all_to_all(outgoing, "node", split_axis=0, concat_axis=0, tiled=True),
        lax.all_to_all(packed_slots, "node", split_axis=0, concat_axis=0, tiled=True),
    )
    got_packed = got_packed.reshape(slot_count)
    got_target = got_packed // blocks % blocks
    bucket = got_packed // (blocks * blocks) * blocks + got_packed % blocks
    sender = jnp.arange(slot_count) // capacity
    chosen = jnp.take(
        group_rows.reshape(shard_count * blocks, tile_edge, feature),
        sender * blocks + got_target,
        axis=0,
    )
    partial_value = jnp.einsum(
        "sij,sid->sjd",
        got_tiles.reshape(slot_count, tile_edge, tile_edge),
        chosen,
        preferred_element_type=jnp.float32,
    )
    partial_value = partial_value.astype(jnp.bfloat16)
    onehot = (bucket[:, None] == jnp.arange(relations * blocks)[None, :]).astype(jnp.bfloat16)
    summed = jnp.einsum(
        "sk,sx->kx",
        onehot,
        partial_value.reshape(slot_count, tile_edge * feature),
        preferred_element_type=jnp.float32,
    )
    aggregated = summed.reshape(relations, row_count, feature).astype(jnp.bfloat16)
    weight_terms = jnp.einsum(
        "vi,rvj->rij", layer_input[0], aggregated, preferred_element_type=jnp.float32
    )
    rel_weight_grad = lax.psum_scatter(weight_terms, "node", scatter_dimension=1, tiled=True)
    own_rows = lax.psum_scatter(
        jnp.einsum("rvj,rij->vi", aggregated, rel_weights, preferred_element_type=jnp.float32),
        "rel",
        scatter_dimension=0,
        tiled=True,
    )
    self_term = jnp.einsum(
        "vj,ij->vi", out_adjoint[0], self_weight, preferred_element_type=jnp.float32
    )
    d_source = (own_rows + self_term).astype(jnp.bfloat16)[None]
    return (rel_weight_grad, d_source)


def solution(mesh):
    return jax.shard_map(
        on_device,
        mesh=mesh,
        in_specs=(
            P("node", "rel", None),
            P("node", None, None),
            P("rel", None, None),
            P(),
            P("rel", "node", None, None),
            P("rel", "node"),
            P("rel", "node"),
            P("rel", "node"),
            P("rel", "node", None),
        ),
        out_specs=(P("rel", "node", None), P("node", "rel", None)),
        check_vma=False,
    )
```

profile of v0, /device:TPU:32, one launch (start us, length us, event | category | flops | bytes accessed | tf_op | source)
XLA Modules:
  0.0 511.2 jit_solution(1792230578648732150)
XLA Ops:
  7.2 0.0 copy-start
  7.2 0.0 all-gather.3.cloned.1.call-start
  7.2 0.7 all-gather.3.cloned.1.call-update
  7.9 0.0 all-gather.5.cloned.1.call-start
  8.0 52.8 %all-gather.3.cloned.1.call-done = bf16[1,1024,512]{2,1,0:T(8,128)(2,1)} async-done(((bf16[1,64,512]{2,1,0:T(8,128)(2,1)}), bf16[1,1024,512]{2,1,0:T(8,128)(2,1)}) %all-gather.3.cloned.1.call-update) | async-done | bytes 1048592 | tf_op jit(solution)/shard_map/all_gather | solution.py:27
  60.8 0.0 all-gather.5.cloned.1.call-update
  60.8 0.9 convert_reduce_fusion
  61.7 0.7 multiply_add_fusion
  62.4 0.7 add_bitcast_fusion
  63.1 0.1 select_reduce_fusion
  63.2 0.7 all_to_all.9
  63.9 7.5 %all-to-all-start = ((s32[16,1,8]{2,1,0:T(1,128)}), s32[16,1,8]{2,1,0:T(1,128)S(1)}, u32[]{:S(2)}, u32[]{:S(2)}) async-start(s32[16,1,8]{2,1,0:T(1,128)} %bitcast.2), calls=%async_computation | async-start | bytes 16384 | tf_op jit(solution)/shard_map/all_to_all | solution.py:52
  71.4 5.2 %fusion.7 = bf16[16,8,128,128]{3,1,2,0:T(8,128)(2,1)} fusion(bf16[8,8,128,128]{3,2,1,0:T(8,128)(2,1)} %bitcast.43, s32[64]{0:T(128)S(1)} %multiply_add_fusion), kind=kOutput, calls=%fused_computation.8 | convolution fusion | flops 270540800 | bytes 6291712 | tf_op jit(solution)/shard_map/dot_general | solution.py:41
  76.6 0.9 all-to-all-done
  77.5 6.3 %all-to-all-start.1 = ((bf16[16,8,128,128]{3,1,2,0:T(8,128)(2,1)}), bf16[16,8,128,128]{3,1,2,0:T(8,128)(2,1)}, u32[]{:S(2)}, u32[]{:S(2)}) async-start(bf16[16,8,128,128]{3,1,2,0:T(8,128)(2,1)} %fusion.7), calls=%async_computation.1 | async-start | bytes 8388608 | tf_op jit(solution)/shard_map/all_to_all | solution.py:51
  83.8 0.0 all-reduce.3.cloned.1.call-start
  83.8 0.5 broadcast.300
  84.4 0.7 reduce.5
  85.0 0.1 reshape.241
  85.1 0.1 reshape.245
  85.3 135.1 %all-to-all-done.1 = bf16[16,8,128,128]{3,1,2,0:T(8,128)(2,1)} async-done(((bf16[16,8,128,128]{3,1,2,0:T(8,128)(2,1)}), bf16[16,8,128,128]{3,1,2,0:T(8,128)(2,1)}, u32[]{:S(2)}, u32[]{:S(2)}) %all-to-all-start.1) | async-done | bytes 4194336 | tf_op jit(solution)/shard_map/all_to_all | solution.py:51
  220.4 6.9 %copy.23 = bf16[16,8,128,128]{2,3,1,0:T(8,128)(2,1)} copy(bf16[16,8,128,128]{3,1,2,0:T(8,128)(2,1)} %all-to-all-done.1) | data formatting | bytes 8388608 | tf_op jit(solution)/shard_map/all_to_all | solution.py:51
  227.3 18.1 %all-gather.5.cloned.1.call-done = bf16[16,1024,512]{2,1,0:T(8,128)(2,1)} async-done(((bf16[1,1024,512]{2,1,0:T(8,128)(2,1)}), bf16[16,1024,512]{2,1,0:T(8,128)(2,1)}) %all-gather.5.cloned.1.call-update) | async-done | bytes 16777232 | tf_op jit(solution)/shard_map/all_gather | solution.py:39
  245.4 14.1 %gather_fusion = bf16[128,128,512]{2,1,0:T(8,128)(2,1)} fusion(bf16[128,128,512]{2,1,0:T(8,128)(2,1)} %bitcast.42, s32[1024]{0:T(1024)S(1)} %pad_clamp_fusion), kind=kCustom, calls=%fused_computation | custom fusion | bytes 33554944 | tf_op jit(solution)/shard_map/jit(_take)/gather | solution.py:58
  259.5 15.7 %fusion.3 = bf16[128,128,512]{2,1,0:T(8,128)(2,1)} fusion(bf16[128,128,128]{1,2,0:T(8,128)(2,1)} %bitcast.41, bf16[128,128,512]{2,1,0:T(8,128)(2,1)} %gather_fusion, pred[128]{0:T(512)(128)(4,1)S(1)} %compare_and_fusion), kind=kOutput, calls=%fused_computation.6 | convolution fusion | flops 2164260864 | bytes 37748864 | tf_op jit(solution)/shard_map/sij,sid->sjd/dot_general | solution.py:63
  275.2 15.8 %copy.29 = bf16[16,8,128,512]{3,1,2,0:T(8,128)(2,1)S(1)} copy(bf16[16,8,128,512]{3,2,1,0:T(8,128)(2,1)} %bitcast.39) | data formatting | bytes 33554432
  291.1 2.6 convolution_convert_fusion
  293.7 2.0 convert_element_type.25
  295.7 0.0 copy-done
  295.7 4.2 convolution_bitcast_fusion.1
  299.9 0.0 copy-start.1
  299.9 4.2 copy.25
  304.1 0.0 all-reduce.3.cloned.1.call-update
  304.2 0.0 copy-start.3
  304.2 0.0 copy-start.2
  304.2 0.0 reduce-scatter.2.cloned.1.call-start
  304.2 0.0 copy-done.1
  304.2 3.8 convolution_bitcast_fusion
  308.1 0.0 reduce-scatter.2.cloned.1.call-update
  308.1 0.0 copy-done.3
  308.1 0.6 dynamic-slice
  309.3 107.4 %all-reduce.3.cloned.1.call-done = f32[2,512,512]{2,0,1:T(2,128)} async-done(((f32[2,512,512]{2,0,1:T(2,128)}), f32[2,512,512]{2,0,1:T(2,128)}) %all-reduce.3.cloned.1.call-update) | async-done | bytes 2097168
  416.8 0.9 constant_dynamic-slice_fusion
  417.7 0.7 copy.26
  418.4 84.3 %reduce-scatter.2.cloned.1.call-done = f32[64,512]{1,0:T(8,128)} async-done(((f32[1024,512]{1,0:T(8,128)}), f32[64,512]{1,0:T(8,128)}) %reduce-scatter.2.cloned.1.call-update) | async-done | bytes 131088 | tf_op jit(solution)/shard_map/reduce_scatter | solution.py:82
  502.7 0.0 copy-done.2
  502.7 2.0 fusion.11
  (4 shorter events, 0.1 us)
Async XLA Ops:
  7.2 288.5 %copy-start = (bf16[1,1024,512]{2,1,0:T(8,128)(2,1)S(1)}, bf16[1,1024,512]{2,1,0:T(8,128)(2,1)}, u32[]{:S(2)}) copy-start(bf16[1,1024,512]{2,1,0:T(8,128)(2,1)} %param.10) | copy-start | bytes 3145732
  7.2 53.6 %all-gather.3.cloned.1.call-start = ((), (), s32[]{:S(2)}) async-start(), calls=%async_computation.3 | async-start | bytes 1114112 | tf_op jit(solution)/shard_map/all_gather | solution.py:27
  7.9 237.5 %all-gather.5.cloned.1.call-start = ((), (), s32[]{:S(2)}) async-start(), calls=%async_computation.4 | async-start | bytes 17825792 | tf_op jit(solution)/shard_map/all_gather | solution.py:39
  63.9 13.6 %all-to-all-start = ((s32[16,1,8]{2,1,0:T(1,128)}), s32[16,1,8]{2,1,0:T(1,128)S(1)}, u32[]{:S(2)}, u32[]{:S(2)}) async-start(s32[16,1,8]{2,1,0:T(1,128)} %bitcast.2), calls=%async_computation | async-start | bytes 16384 | tf_op jit(solution)/shard_map/all_to_all | solution.py:52
  77.5 142.9 %all-to-all-start.1 = ((bf16[16,8,128,128]{3,1,2,0:T(8,128)(2,1)}), bf16[16,8,128,128]{3,1,2,0:T(8,128)(2,1)}, u32[]{:S(2)}, u32[]{:S(2)}) async-start(bf16[16,8,128,128]{3,1,2,0:T(8,128)(2,1)} %fusion.7), calls=%async_computation.1 | async-start | bytes 8388608 | tf_op jit(solution)/shard_map/all_to_all | solution.py:51
  83.8 333.0 %all-reduce.3.cloned.1.call-start = ((), (), s32[]{:S(2)}) async-start(), calls=%async_computation.6 | async-start | bytes 4194304
  299.9 4.4 copy-start.1
  304.2 3.9 copy-start.3
  304.2 198.5 %copy-start.2 = (bf16[1,64,512]{2,1,0:T(8,128)(2,1)S(1)}, bf16[1,64,512]{2,1,0:T(8,128)(2,1)}, u32[]{:S(2)}) copy-start(bf16[1,64,512]{2,1,0:T(8,128)(2,1)} %param.9) | copy-start | bytes 196612
  304.2 198.5 %reduce-scatter.2.cloned.1.call-start = ((), (), s32[]{:S(2)}) async-start(), calls=%async_computation.5 | async-start | bytes 2228224 | tf_op jit(solution)/shard_map/reduce_scatter | solution.py:82
Sparse Core Ops, SparseCore 0:
  10.4 50.3 all-gather.2
  62.6 182.7 all-gather.4
  304.3 112.4 all-reduce.2
  420.2 82.4 reduce-scatter.1
where the time goes:
time: 512 us; the launch traced here: 511 us
  waiting for transfers between devices  399 us (78%)
  local copies, waits for them, and re-layouts  46.6 us (9%)
  matrix products  33.5 us (7%)
  between operations  14.5 us (3%)
  starting transfers between devices  13.9 us (3%)
    all_to_all x1, waiting for transfers between devices, on_device(): lax.all_to_all(outgoing, 'node', split_axis=0, concat_axis=0, tiled=True)  135 us
    unnamed x5, waiting for transfers between devices  108 us
    reduce_scatter x1, waiting for transfers between devices, on_device(): lax.psum_scatter(jnp.einsum('rvj,rij->vi', aggregated, rel_weights, prefe...  84.3 us
    all_gather x1, waiting for transfers between devices, on_device(): adjoint = lax.all_gather(out_adjoint, 'rel', axis=1, tiled=True)[0]  52.8 us
    all_gather x1, waiting for transfers between devices, on_device(): group_rows = lax.all_gather(adjoint[None], 'node', axis=0, tiled=True)  18.1 us
    unnamed x12, local copies, waits for them, and re-layouts  18.1 us
    dot_general x1, matrix products, on_device(): jnp.einsum('sij,sid->sjd', got_tiles.reshape(slot_count, tile_edge, tile_...  15.7 us
    gather x1, local copies, waits for them, and re-layouts, on_device(): jnp.take(group_rows.reshape(shard_count * blocks, tile_edge, feature), se...  14.1 us
  transfers between devices with their start and end apart: 6, of which 6 were waited for; matrix products, arithmetic and copies ran while one was open for 4% of the time, Pallas kernels for 0%

commit v1 on v0

--- a/solution.py
+++ b/solution.py
@@ -36,7 +36,13 @@
     slot_of = owners * capacity + position
     placed = jnp.arange(slot_count)[:, None] == slot_of[None, :]
     placing = placed.astype(jnp.bfloat16)
-    group_rows = lax.all_gather(adjoint[None], "node", axis=0, tiled=True)
+    chunk = adjoint[None]
+    group_rows = jnp.concatenate(
+        lax.all_to_all(
+            jnp.stack([chunk for _ in range(lax.axis_size("node"))], axis=0), "node", 0, 0
+        ),
+        axis=0,
+    )
     packed = relation * (blocks * blocks) + target * blocks + source
     outgoing = jnp.dot(
         placing,

time: 512 us -> 767 us (1.50)
  waiting for transfers between devices: 399 us -> 640 us
  starting transfers between devices: 13.9 us -> 21.8 us
    all_to_all x0 -> x1, waiting for transfers between devices: none -> 354 us  [on_device(): lax.all_to_all(jnp.stack([chunk for _ in range(lax.axis_size('node'))], a...]
    all_to_all x1, waiting for transfers between devices: 135 us -> 40.3 us  [on_device(): lax.all_to_all(outgoing, 'node', split_axis=0, concat_axis=0, tiled=True)]
    all_gather x1 -> x0, waiting for transfers between devices: 18.1 us -> none  [on_device(): group_rows = lax.all_gather(adjoint[None], 'node', axis=0, tiled=True)]
    unnamed x5 -> x4, waiting for transfers between devices: 108 us -> 109 us
  transfers between devices with their start and end apart: 6 -> 6, of which waited for: 6 -> 6; matrix products, arithmetic and copies ran while one was open for 4% -> 3% of each run, Pallas kernels for 0% -> 0%
where the time goes in v1:
time: 767 us
  waiting for transfers between devices  640 us (83%)
  local copies, waits for them, and re-layouts  53.3 us (7%)
  matrix products  33.5 us (4%)
  starting transfers between devices  21.8 us (3%)
  between operations  14.5 us (2%)
    all_to_all x1, waiting for transfers between devices, on_device(): lax.all_to_all(jnp.stack([chunk for _ in range(lax.axis_size('node'))], a...  354 us
    unnamed x4, waiting for transfers between devices  109 us
    reduce_scatter x1, waiting for transfers between devices, on_device(): lax.psum_scatter(jnp.einsum('rvj,rij->vi', aggregated, rel_weights, prefe...  84.4 us
    all_gather x1, waiting for transfers between devices, on_device(): adjoint = lax.all_gather(out_adjoint, 'rel', axis=1, tiled=True)[0]  51.4 us
    all_to_all x1, waiting for transfers between devices, on_device(): lax.all_to_all(outgoing, 'node', split_axis=0, concat_axis=0, tiled=True)  40.3 us
    unnamed x12, local copies, waits for them, and re-layouts  18.1 us
    dot_general x1, matrix products, on_device(): jnp.einsum('sij,sid->sjd', got_tiles.reshape(slot_count, tile_edge, tile_...  15.7 us
  transfers between devices with their start and end apart: 6, of which 6 were waited for; matrix products, arithmetic and copies ran while one was open for 3% of the time, Pallas kernels for 0%

profile of v1, /device:TPU:32, one launch (start us, length us, event | category | flops | bytes accessed | tf_op | source)
XLA Modules:
  0.0 766.7 jit_solution(11467968465472710550)
XLA Ops:
  7.2 0.0 copy-start
  7.2 0.9 convert_reduce_fusion
  8.1 0.7 multiply_add_fusion
  8.8 0.7 add_bitcast_fusion
  9.5 0.1 select_reduce_fusion
  9.6 0.7 all_to_all.12
  10.3 8.6 %all-to-all-start = ((s32[16,1,8]{2,1,0:T(1,128)}), s32[16,1,8]{2,1,0:T(1,128)S(1)}, u32[]{:S(2)}, u32[]{:S(2)}) async-start(s32[16,1,8]{2,1,0:T(1,128)} %bitcast.2), calls=%async_computation | async-start | bytes 16384 | tf_op jit(solution)/shard_map/all_to_all | solution.py:58
  18.9 5.1 fusion.7
  24.0 1.0 all-to-all-done
  25.0 6.3 all-to-all-start.1
  31.2 0.0 all-gather.2.cloned.1.call-start
  31.3 0.7 all-gather.2.cloned.1.call-update
  32.0 51.4 %all-gather.2.cloned.1.call-done = bf16[1,1024,512]{2,1,0:T(8,128)(2,1)} async-done(((bf16[1,64,512]{2,1,0:T(8,128)(2,1)}), bf16[1,1024,512]{2,1,0:T(8,128)(2,1)}) %all-gather.2.cloned.1.call-update) | async-done | bytes 1048592 | tf_op jit(solution)/shard_map/all_gather | solution.py:27
  83.4 40.3 %all-to-all-done.1 = bf16[16,8,128,128]{3,1,2,0:T(8,128)(2,1)} async-done(((bf16[16,8,128,128]{3,1,2,0:T(8,128)(2,1)}), bf16[16,8,128,128]{3,1,2,0:T(8,128)(2,1)}, u32[]{:S(2)}, u32[]{:S(2)}) %all-to-all-start.1) | async-done | bytes 4194336 | tf_op jit(solution)/shard_map/all_to_all | solution.py:57
  123.7 6.8 stack.3
  130.5 6.9 all-to-all-start.2
  137.3 0.0 all-reduce.3.cloned.1.call-start
  137.4 0.5 broadcast.303
  137.9 0.7 reduce.5
  138.6 0.1 reshape.241
  138.7 0.1 reshape.244
  138.8 6.8 copy.23
  145.7 354.5 %all-to-all-done.2 = bf16[16,1,1024,512]{3,2,1,0:T(8,128)(2,1)} async-done(((bf16[16,1,1024,512]{3,2,1,0:T(8,128)(2,1)}), bf16[16,1,1024,512]{3,2,1,0:T(8,128)(2,1)}, u32[]{:S(2)}, u32[]{:S(2)}) %all-to-all-start.2) | async-done | bytes 16777248 | tf_op jit(solution)/shard_map/all_to_all | solution.py:41
  500.2 14.1 %gather_fusion = bf16[128,128,512]{2,1,0:T(8,128)(2,1)} fusion(bf16[128,128,512]{2,1,0:T(8,128)(2,1)} %bitcast.6, s32[1024]{0:T(1024)S(1)} %pad_clamp_fusion), kind=kCustom, calls=%fused_computation | custom fusion | bytes 33554944 | tf_op jit(solution)/shard_map/jit(_take)/gather | solution.py:64
  514.2 15.7 %fusion.3 = bf16[128,128,512]{2,1,0:T(8,128)(2,1)} fusion(bf16[128,128,128]{1,2,0:T(8,128)(2,1)} %bitcast.42, bf16[128,128,512]{2,1,0:T(8,128)(2,1)} %gather_fusion, pred[128]{0:T(512)(128)(4,1)S(1)} %compare_and_fusion), kind=kOutput, calls=%fused_computation.6 | convolution fusion | flops 2164260864 | bytes 37748864 | tf_op jit(solution)/shard_map/sij,sid->sjd/dot_general | solution.py:69
  530.0 15.8 %copy.29 = bf16[16,8,128,512]{3,1,2,0:T(8,128)(2,1)S(1)} copy(bf16[16,8,128,512]{3,2,1,0:T(8,128)(2,1)} %bitcast.40) | data formatting | bytes 33554432
  545.8 2.6 convolution_convert_fusion
  548.5 2.0 convert_element_type.25
  550.5 0.0 copy-done
  550.5 4.2 convolution_bitcast_fusion.1
  554.6 0.0 copy-start.1
  554.6 4.3 copy.25
  558.9 0.0 all-reduce.3.cloned.1.call-update
  558.9 0.0 copy-start.3
  558.9 0.0 copy-start.2
  558.9 0.0 reduce-scatter.2.cloned.1.call-start
  559.0 0.0 copy-done.1
  559.0 3.8 convolution_bitcast_fusion
  562.8 0.0 reduce-scatter.2.cloned.1.call-update
  562.9 0.0 copy-done.3
  562.9 0.6 dynamic-slice
  564.1 108.0 %all-reduce.3.cloned.1.call-done = f32[2,512,512]{2,0,1:T(2,128)} async-done(((f32[2,512,512]{2,0,1:T(2,128)}), f32[2,512,512]{2,0,1:T(2,128)}) %all-reduce.3.cloned.1.call-update) | async-done | bytes 2097168
  672.2 0.9 constant_dynamic-slice_fusion
  673.1 0.7 copy.26
  673.7 84.4 %reduce-scatter.2.cloned.1.call-done = f32[64,512]{1,0:T(8,128)} async-done(((f32[1024,512]{1,0:T(8,128)}), f32[64,512]{1,0:T(8,128)}) %reduce-scatter.2.cloned.1.call-update) | async-done | bytes 131088 | tf_op jit(solution)/shard_map/reduce_scatter | solution.py:88
  758.2 0.0 copy-done.2
  758.2 2.0 fusion.11
  (4 shorter events, 0.1 us)
Async XLA Ops:
  7.2 543.3 %copy-start = (bf16[1,1024,512]{2,1,0:T(8,128)(2,1)S(1)}, bf16[1,1024,512]{2,1,0:T(8,128)(2,1)}, u32[]{:S(2)}) copy-start(bf16[1,1024,512]{2,1,0:T(8,128)(2,1)} %param.10) | copy-start | bytes 3145732
  10.3 14.7 %all-to-all-start = ((s32[16,1,8]{2,1,0:T(1,128)}), s32[16,1,8]{2,1,0:T(1,128)S(1)}, u32[]{:S(2)}, u32[]{:S(2)}) async-start(s32[16,1,8]{2,1,0:T(1,128)} %bitcast.2), calls=%async_computation | async-start | bytes 16384 | tf_op jit(solution)/shard_map/all_to_all | solution.py:58
  25.0 98.7 %all-to-all-start.1 = ((bf16[16,8,128,128]{3,1,2,0:T(8,128)(2,1)}), bf16[16,8,128,128]{3,1,2,0:T(8,128)(2,1)}, u32[]{:S(2)}, u32[]{:S(2)}) async-start(bf16[16,8,128,128]{3,1,2,0:T(8,128)(2,1)} %fusion.7), calls=%async_computation.1 | async-start | bytes 8388608 | tf_op jit(solution)/shard_map/all_to_all | solution.py:57
  31.2 52.1 %all-gather.2.cloned.1.call-start = ((), (), s32[]{:S(2)}) async-start(), calls=%async_computation.4 | async-start | bytes 1114112 | tf_op jit(solution)/shard_map/all_gather | solution.py:27
  130.5 369.7 %all-to-all-start.2 = ((bf16[16,1,1024,512]{3,2,1,0:T(8,128)(2,1)}), bf16[16,1,1024,512]{3,2,1,0:T(8,128)(2,1)}, u32[]{:S(2)}, u32[]{:S(2)}) async-start(bf16[16,1,1024,512]{3,2,1,0:T(8,128)(2,1)} %stack.3), calls=%async_computation.2 | async-start | bytes 33554432 | tf_op jit(solution)/shard_map/all_to_all | solution.py:41
  137.3 534.8 %all-reduce.3.cloned.1.call-start = ((), (), s32[]{:S(2)}) async-start(), calls=%async_computation.6 | async-start | bytes 4194304
  554.6 4.4 copy-start.1
  558.9 3.9 copy-start.3
  558.9 199.3 %copy-start.2 = (bf16[1,64,512]{2,1,0:T(8,128)(2,1)S(1)}, bf16[1,64,512]{2,1,0:T(8,128)(2,1)}, u32[]{:S(2)}) copy-start(bf16[1,64,512]{2,1,0:T(8,128)(2,1)} %param.9) | copy-start | bytes 196612
  558.9 199.2 %reduce-scatter.2.cloned.1.call-start = ((), (), s32[]{:S(2)}) async-start(), calls=%async_computation.5 | async-start | bytes 2228224 | tf_op jit(solution)/shard_map/reduce_scatter | solution.py:88
Sparse Core Ops, SparseCore 0:
  34.5 48.8 all-gather.1
  559.0 113.0 all-reduce.2
  675.7 82.4 reduce-scatter.1
